TPU v7x, 32 devices: a whole 2x2x4 slice. The times are simulated.
32 devices in a mesh: parts: 2 (over y), region: 2 (over x), dev: 4 (over z), pair: 2 (over core).
Axes of the slice: x: 2, y: 2, z: 4, core: 2. Of those that a mesh axis runs over, the one named last changes fastest.
Arguments:
- observed_rates: bfloat16 [32, 4096], P(('parts', 'region', 'dev', 'pair')), parts along dimension 0, may hold values from -0.94921875 to 0.94921875
- block_values: bfloat16 [16, 1024, 1024], P(('parts', 'region', 'dev')), parts along dimension 0, may hold values from -0.125 to 0.125
- block_row: int32 [16], P('parts'), parts along dimension 0, may hold values from 0 to 3, as said below
- block_col: int32 [16], P('parts'), parts along dimension 0, may hold values from 0 to 3, as said below
- deal_list: int32 [16], P('parts'), parts along dimension 0, may hold values from 0 to 7, each once
- scale_index: int32 [16, 8], P(('parts', 'region', 'dev')), parts along dimension 0, may hold values from 0 to 15
- scale_table: float32 [32], P('parts'), parts along dimension 0, may hold values from 0.5 to 2
Outputs:
- errors: bfloat16 [32, 4096], P(('parts', 'region', 'dev', 'pair')), parts along dimension 0
- block_grads: bfloat16 [16, 1024, 1024], P(('parts', 'region', 'dev'), 'pair'), parts along dimension 0
There are 2 independent parts, one for each index of `parts`. A program takes and returns all parts, laid end to end along the dimension named above; each array names one. Nothing has to cross between parts.
Inputs may be any that keep to these rules, and one draw needn't show every extreme that they name: Every block row and every block column holds exactly two blocks, and no pair (block_row, block_col) repeats. Every block column holds exactly two blocks, and no pair (block_row, block_col) repeats.
All inputs are finite; a program needn't handle non-finite values.
Results may differ from a plain program's by a relative error of at most 0.006.
Values may be sent and summed in bfloat16 or wider, within the bound.
A program may use at most 64 MiB of HBM per device.

v0:
```python
import math

import jax
import jax.numpy as jnp
from jax import lax
from jax.sharding import PartitionSpec as P


def from_behind(value, axis, by):
    size = lax.axis_size(axis)
    pairs = [(i, i + by) for i in range(size) if 0 <= i + by < size]
    return lax.ppermute(value, axis, pairs)


def contract_time(signal_part, source_part):
    return lax.dot_general(
        signal_part, source_part, (((0,), (0,)), ((), ())), preferred_element_type=jnp.float32
    )


def shards(observed_rates, block_values, block_row, block_col, deal_list, scale_index, scale_table):
    blocks_all = lax.axis_size(("region", "dev"))
    step_dev = observed_rates.shape[0]
    neurons = observed_rates.shape[1]
    block = block_values.shape[1]
    block_rows = neurons // block
    steps_all = step_dev * lax.axis_size(("region", "dev", "pair"))
    row_of = block_row[deal_list]
    col_of = block_col[deal_list]
    panels = observed_rates.reshape(step_dev, block_rows, block)
    outgoing = jnp.take(panels, col_of, axis=1)
    incoming = lax.all_to_all(outgoing, ("region", "dev"), split_axis=1, concat_axis=0, tiled=True)
    source = incoming.reshape(step_dev * blocks_all, block)
    matches = scale_index[0][:, None] == jnp.arange(scale_table.shape[0])[None, :]
    group_scale = jnp.sum(jnp.where(matches, scale_table[None, :], 0.0), axis=1)
    column_scale = jnp.repeat(group_scale, 128)
    effective = (block_values[0].astype(jnp.float32) * column_scale[None, :]).astype(jnp.bfloat16)
    partial_value = lax.dot_general(
        source, effective, (((1,), (1,)), ((), ())), preferred_element_type=jnp.float32
    )
    returned = lax.all_to_all(
        partial_value.reshape(blocks_all, step_dev, block),
        ("region", "dev"),
        split_axis=0,
        concat_axis=0,
        tiled=True,
    )
    row_hits = (row_of[:, None] == jnp.arange(block_rows)[None, :]).astype(jnp.float32)
    currents = jnp.einsum("kts,kr->trs", returned, row_hits, precision=lax.Precision.HIGHEST)
    predicted = jnp.tanh(currents).reshape(step_dev, neurons)
    following = from_behind(observed_rates, ("region", "dev", "pair"), -1)
    target = jnp.concatenate([observed_rates[1:], following], axis=0).astype(jnp.float32)
    position = lax.axis_index(("region", "dev", "pair")) * step_dev + jnp.arange(step_dev)
    valid = (position < steps_all - 1)[:, None]
    mismatch = jnp.where(valid, predicted - target, 0.0)
    errors = mismatch.astype(jnp.bfloat16)
    signal = (mismatch * (1.0 - predicted * predicted) * (1.0 / math.sqrt(steps_all))).astype(
        jnp.bfloat16
    )
    outgoing_signal = jnp.take(signal.reshape(step_dev, block_rows, block), row_of, axis=1)
    arrived = lax.all_to_all(
        outgoing_signal, ("region", "dev"), split_axis=1, concat_axis=0, tiled=True
    ).reshape(step_dev * blocks_all, block)
    block_grads = lax.psum_scatter(
        contract_time(arrived, source) * column_scale[None, :],
        "pair",
        scatter_dimension=0,
        tiled=True,
    ).astype(jnp.bfloat16)
    return (errors, block_grads[None])


def solution(mesh):
    return jax.shard_map(
        shards,
        mesh=mesh,
        in_specs=(
            P(("parts", "region", "dev", "pair"), None),
            P(("parts", "region", "dev"), None, None),
            P("parts"),
            P("parts"),
            P("parts"),
            P(("parts", "region", "dev"), None),
            P("parts"),
        ),
        out_specs=(
            P(("parts", "region", "dev", "pair"), None),
            P(("parts", "region", "dev"), "pair", None),
        ),
        check_vma=False,
    )
```

profile of v0, /device:TPU:0, one launch (start us, length us, event | category | flops | bytes accessed | tf_op | source)
XLA Modules:
  0.0 73.4 jit_solution(1900276713919240263)
XLA Ops:
  7.2 0.0 copy-start
  7.2 1.3 %collective-permute-start = (bf16[1,4096]{1,0:T(2,128)(2,1)}, bf16[1,4096]{1,0:T(2,128)(2,1)S(1)}, u32[]{:S(2)}, u32[]{:S(2)}) collective-permute-start(bf16[1,4096]{1,0:T(2,128)(2,1)} %param.9), channel_id=1, source_target_pairs={{1,0},{2,1},{3,2},{4,3},{5,4},{6,5},{7,6},{8,7},{9,8},{10,9},{11,1... | collective-permute-start | bytes 24584 | tf_op jit(solution)/shard_map/ppermute | solution.py:12
  8.5 0.7 compare_select_fusion.2
  9.1 0.0 copy-done
  9.1 0.6 gather_fusion.1
  9.8 0.8 %reduce = bf16[4096]{0:T(1024)(128)(2,1)S(1)} reduce(bf16[1,4096]{1,0:T(2,128)(2,1)} %param.9, bf16[]{:T(256)} %constant.40), dimensions={0}, to_apply=%param.9.reduce_sub_computation | reduce | bytes 16386 | tf_op args[0]
  10.6 0.6 gather_fusion.2
  11.2 0.1 bitcast_select_fusion.1
  11.3 0.6 broadcast.103
  11.9 0.8 %reduce.3 = bf16[8,1024]{1,0:T(8,128)(2,1)S(1)} reduce(bf16[8,1,1024]{2,1,0:T(2,128)(2,1)S(1)} %bitcast.43, bf16[]{:T(256)} %broadcast.103), dimensions={1}, to_apply=%bitcast.38.reduce_sub_computation | reduce | bytes 32770
  12.7 0.6 reshape.160
  13.3 7.9 %all-to-all-start = ((bf16[8,2,512]{2,1,0:T(2,128)(2,1)}), bf16[8,2,512]{2,1,0:T(2,128)(2,1)S(1)}, u32[]{:S(2)}, u32[]{:S(2)}) async-start(bf16[8,2,512]{2,1,0:T(2,128)(2,1)} %reshape.160), calls=%async_computation | async-start | bytes 32768 | tf_op jit(solution)/shard_map/all_to_all | solution.py:32
  21.2 0.9 %select_reduce_fusion = f32[8]{0:T(128)S(1)} fusion(f32[16]{0:T(128)} %param.15, s32[8]{0:T(128)} %bitcast.46), kind=kLoop, calls=%fused_computation.28 | loop fusion | flops 376 | bytes 128 | tf_op jit(solution)/shard_map/reduce_sum | solution.py:35
  22.0 0.1 broadcast_bitcast_fusion
  22.1 1.3 %gather_fusion = s32[8]{0:T(128)S(1)} fusion(s32[8]{0:T(128)} %param.11, s32[1024]{0:T(1024)S(1)} %pad_clamp_fusion.2), kind=kCustom, calls=%fused_computation.2 | custom fusion | bytes 96 | tf_op jit(solution)/shard_map/gather | solution.py:28
  23.4 4.3 %all-to-all-done = bf16[8,2,512]{2,1,0:T(2,128)(2,1)S(1)} async-done(((bf16[8,2,512]{2,1,0:T(2,128)(2,1)}), bf16[8,2,512]{2,1,0:T(2,128)(2,1)S(1)}, u32[]{:S(2)}, u32[]{:S(2)}) %all-to-all-start) | async-done | bytes 16416 | tf_op jit(solution)/shard_map/all_to_all | solution.py:32
  27.8 2.2 %fusion.4 = f32[8,1,1024]{2,0,1:T(8,128)S(1)} fusion(bf16[1,1024,1024]{2,1,0:T(8,128)(2,1)} %param.10, f32[1024]{0:T(1024)S(1)} %broadcast_bitcast_fusion, bf16[1,8,1024]{2,0,1:T(2,128)(2,1)S(1)} %bitcast.41), kind=kOutput, calls=%fused_computation.9 | convolution fusion | flops 19922944 | bytes 2150400 | tf_op jit(solution)/shard_map/dot_general | solution.py:38
  30.0 0.7 copy.16
  30.7 3.3 %all-to-all-start.1 = ((f32[8,1,1024]{2,1,0:T(1,128)}), f32[8,1,1024]{2,1,0:T(1,128)S(1)}, u32[]{:S(2)}, u32[]{:S(2)}) async-start(f32[8,1,1024]{2,1,0:T(1,128)} %copy.16), calls=%async_computation.1 | async-start | bytes 65536 | tf_op jit(solution)/shard_map/all_to_all | solution.py:41
  34.0 0.0 reduce-scatter.2.cloned.1.call-start
  34.1 6.6 %all-to-all-done.1 = f32[8,1,1024]{2,1,0:T(1,128)S(1)} async-done(((f32[8,1,1024]{2,1,0:T(1,128)}), f32[8,1,1024]{2,1,0:T(1,128)S(1)}, u32[]{:S(2)}, u32[]{:S(2)}) %all-to-all-start.1) | async-done | bytes 32800 | tf_op jit(solution)/shard_map/all_to_all | solution.py:41
  40.7 0.3 fusion.7
  41.0 0.0 collective-permute-done
  41.0 0.1 convert_reduce_fusion
  41.1 0.6 gather_fusion.3
  41.7 0.1 bitcast_select_fusion
  41.8 0.8 %reduce.4 = bf16[8,1024]{1,0:T(8,128)(2,1)S(1)} reduce(bf16[8,1,1024]{2,1,0:T(2,128)(2,1)S(1)} %bitcast.44, bf16[]{:T(256)} %broadcast.103), dimensions={1}, to_apply=%bitcast.37.reduce_sub_computation | reduce | bytes 32770
  42.6 9.0 %all_to_all.23 = bf16[8,2,512]{2,1,0:T(2,128)(2,1)S(1)} all-to-all(bf16[8,2,512]{2,1,0:T(2,128)(2,1)S(1)} %reshape.162), channel_id=1, replica_groups=mesh['parts'=2,'region'=2,'dev'=4,'pair'=2] {'region','dev'}, dimensions={0} | all-to-all | bytes 32768 | tf_op jit(solution)/shard_map/all_to_all | solution.py:61
  51.6 2.7 %convolution_multiply_fusion = f32[1024,1024]{1,0:T(8,128)} fusion(f32[1024]{0:T(1024)S(1)} %broadcast_bitcast_fusion, bf16[1,8,1024]{2,0,1:T(2,128)(2,1)S(1)} %bitcast.45, bf16[1,8,1024]{2,0,1:T(2,128)(2,1)S(1)} %bitcast.42), kind=kOutput, calls=%fused_computation.5 | convolution fusion | flops 17825792 | bytes 4231168 | tf_op jit(solution)/shard_map/dot_general | solution.py:16
  54.3 0.0 reduce-scatter.2.cloned.1.call-update
  54.3 0.6 fusion.17
  54.9 8.9 %reduce-scatter.2.cloned.1.call-done = f32[512,1024]{1,0:T(8,128)} async-done(((f32[1024,1024]{1,0:T(8,128)}), f32[512,1024]{1,0:T(8,128)}) %reduce-scatter.2.cloned.1.call-update) | async-done | bytes 2097168 | tf_op jit(solution)/shard_map/reduce_scatter | solution.py:64
  63.8 2.7 %convert_bitcast_fusion = bf16[1,512,1024]{2,1,0:T(8,128)(2,1)} fusion(f32[512,1024]{1,0:T(8,128)} %reduce-scatter.2.cloned.1.call-done), kind=kLoop, calls=%fused_computation.12 | loop fusion | flops 524288 | bytes 3145728 | tf_op jit(solution)/shard_map/broadcast_in_dim | solution.py:70
  (15 shorter events, 0.2 us)
Async XLA Ops:
  7.2 2.0 %copy-start = (s32[8]{0:T(128)S(1)}, s32[8]{0:T(128)}, u32[]{:S(2)}) copy-start(s32[8]{0:T(128)} %param.12) | copy-start | bytes 100
  7.2 33.8 %collective-permute-start = (bf16[1,4096]{1,0:T(2,128)(2,1)}, bf16[1,4096]{1,0:T(2,128)(2,1)S(1)}, u32[]{:S(2)}, u32[]{:S(2)}) collective-permute-start(bf16[1,4096]{1,0:T(2,128)(2,1)} %param.9), channel_id=1, source_target_pairs={{1,0},{2,1},{3,2},{4,3},{5,4},{6,5},{7,6},{8,7},{9,8},{10,9},{11,1... | collective-permute-start | bytes 24584 | tf_op jit(solution)/shard_map/ppermute | solution.py:12
  13.3 14.5 %all-to-all-start = ((bf16[8,2,512]{2,1,0:T(2,128)(2,1)}), bf16[8,2,512]{2,1,0:T(2,128)(2,1)S(1)}, u32[]{:S(2)}, u32[]{:S(2)}) async-start(bf16[8,2,512]{2,1,0:T(2,128)(2,1)} %reshape.160), calls=%async_computation | async-start | bytes 32768 | tf_op jit(solution)/shard_map/all_to_all | solution.py:32
  30.7 10.0 %all-to-all-start.1 = ((f32[8,1,1024]{2,1,0:T(1,128)}), f32[8,1,1024]{2,1,0:T(1,128)S(1)}, u32[]{:S(2)}, u32[]{:S(2)}) async-start(f32[8,1,1024]{2,1,0:T(1,128)} %copy.16), calls=%async_computation.1 | async-start | bytes 65536 | tf_op jit(solution)/shard_map/all_to_all | solution.py:41
  34.0 29.8 %reduce-scatter.2.cloned.1.call-start = ((), (), s32[]{:S(2)}) async-start(), calls=%async_computation.4 | async-start | bytes 6291456 | tf_op jit(solution)/shard_map/reduce_scatter | solution.py:64
Sparse Core Ops, SparseCore 0:
  54.4 9.3 reduce-scatter.1
where the time goes:
time: 73.8 us; the launch traced here: 73.4 us
  waiting for transfers between devices  19.8 us (27%)
  between operations  14.2 us (19%)
  starting transfers between devices  12.6 us (17%)
  blocking collectives  8.96 us (12%)
  other arithmetic  7.47 us (10%)
  local copies, waits for them, and re-layouts  5.19 us (7%)
  matrix products  5.19 us (7%)
    all_to_all x1, blocking collectives, shards(): lax.all_to_all(outgoing_signal, ('region', 'dev'), split_axis=1, concat_a...  8.96 us
    reduce_scatter x1, waiting for transfers between devices, shards(): lax.psum_scatter(contract_time(arrived, source) * column_scale[None, :],...  8.88 us
    all_to_all x1, starting transfers between devices, shards(): lax.all_to_all(outgoing, ('region', 'dev'), split_axis=1, concat_axis=0,...  7.88 us
    all_to_all x1, waiting for transfers between devices, shards(): lax.all_to_all(partial_value.reshape(blocks_all, step_dev, block), ('regi...  6.6 us
    all_to_all x1, waiting for transfers between devices, shards(): lax.all_to_all(outgoing, ('region', 'dev'), split_axis=1, concat_axis=0,...  4.34 us
    all_to_all x1, starting transfers between devices, shards(): lax.all_to_all(partial_value.reshape(blocks_all, step_dev, block), ('regi...  3.34 us
    broadcast_in_dim x1, other arithmetic, shards(): return (errors, block_grads[None])  2.72 us
    dot_general x1, matrix products, contract_time(): lax.dot_general(signal_part, source_part, (((0,), (0,)), ((), ())), prefe...  2.68 us
  transfers between devices with their start and end apart: 4, of which 3 were waited for; matrix products, arithmetic and copies ran while one was open for 15% of the time, Pallas kernels for 0%

commit v1 on v0

v1 whole, which is shorter than its diff:
```python
import functools
import math

import jax
import jax.numpy as jnp
from jax import lax
from jax.experimental import pallas as pl
from jax.experimental.pallas import tpu as pltpu
from jax.sharding import PartitionSpec as P

LANES = 128
MESH = pl.DeviceIdType.MESH


def repeat(count, body):
    if count <= 32:
        for i in range(count):
            body(i)
    else:
        lax.fori_loop(0, count, lambda i, carry: (body(i), carry)[1], 0)


def exchange_kernel(
    regions, devs, pairs,
    rates_ref, values_ref, row_ref, col_ref, deal_ref, index_ref, table_ref,
    signal_ref, source_ref, errors_ref, scale_ref,
    panels, panels16, following, out1, rates_in, block, work, out2, partials_in,
    mismatches, gradients, out3, signal_in,
    block_sem, send1, recv1, send_next, recv_next, send_pair, recv_pair,
    send2, recv2, send3, recv3,
):
    slots = regions * devs
    steps = slots * pairs
    rows = panels.shape[0]
    size = block.shape[0]
    group = size // LANES
    c = lax.axis_index("pair")
    q = lax.axis_index("region") * devs + lax.axis_index("dev")
    me = c * slots + q

    def at(slot, core):
        return {"region": slot // devs, "dev": slot % devs, "pair": core}

    load = pltpu.make_async_copy(values_ref.at[0], block, block_sem)
    load.start()

    barrier = pltpu.get_barrier_semaphore()

    def greet(i):
        other = lax.rem(me + 1 + i, steps)
        pl.semaphore_signal(
            barrier, inc=1, device_id=at(lax.rem(other, slots), other // slots), device_id_type=MESH
        )

    repeat(steps - 1, greet)

    def spread(i):
        lanes = pl.ds(i * LANES, LANES) if isinstance(i, int) else pl.ds(
            pl.multiple_of(i * LANES, LANES), LANES)
        panels[i // 8, pl.ds(i % 8, 1), :] = rates_ref[:, lanes].astype(jnp.float32)

    repeat(rows * 8, spread)
    panels16[...] = panels[...].astype(jnp.bfloat16)

    def pick(k):
        out1[k] = panels[col_ref[deal_ref[k]]].astype(jnp.bfloat16)

    repeat(slots, pick)
    rates_in[me] = panels[col_ref[deal_ref[q]]].astype(jnp.bfloat16)
    pl.semaphore_wait(barrier, steps - 1)

    def rates_copy(to, frm):
        return pltpu.make_async_remote_copy(
            src_ref=out1.at[to], dst_ref=rates_in.at[c * slots + frm],
            send_sem=send1.at[to], recv_sem=recv1.at[frm],
            device_id=at(to, c), device_id_type=MESH,
        )

    def send_rates(i):
        rates_copy(lax.rem(q + 1 + i, slots), q).start()

    repeat(slots - 1, send_rates)
    before = lax.rem(q * pairs + c + steps - 1, steps)
    next_copy = pltpu.make_async_remote_copy(
        src_ref=panels16, dst_ref=following, send_sem=send_next, recv_sem=recv_next,
        device_id=at(before // pairs, lax.rem(before, pairs)), device_id_type=MESH,
    )
    next_copy.start()

    for g in range(group):
        scale_ref[:, g * LANES:(g + 1) * LANES] = jnp.full(
            (1, LANES), table_ref[index_ref[0, g]], jnp.float32)
    load.wait()
    chunk = 64

    @pl.loop(0, size // chunk)
    def _(i):
        part = pl.ds(pl.multiple_of(i * chunk, chunk), chunk)
        block[part, :] = (block[part, :].astype(jnp.float32) * scale_ref[...]).astype(jnp.bfloat16)

    def wait_rates(i):
        rates_copy(lax.rem(q + 1 + i, slots), lax.rem(q + 1 + i, slots)).wait_recv()

    repeat(slots - 1, wait_rates)
    mine = pl.ds(c * slots, slots)
    pair_copy = pltpu.make_async_remote_copy(
        src_ref=rates_in.at[mine], dst_ref=rates_in.at[mine],
        send_sem=send_pair, recv_sem=recv_pair, device_id=at(q, 1 - c), device_id_type=MESH,
    )
    pair_copy.start()
    work[pl.ds(0, slots * 8), :] = rates_in[mine].astype(jnp.float32).reshape(slots * 8, LANES)
    source = jnp.concatenate(
        [work[pl.ds(j, slots, stride=8), :] for j in range(group)], axis=1).astype(jnp.bfloat16)
    partial_value = lax.dot_general(
        source, block[...], (((1,), (1,)), ((), ())), preferred_element_type=jnp.float32)
    for j in range(group):
        out2[pl.ds(j, slots, stride=8), :] = partial_value[:, j * LANES:(j + 1) * LANES]

    def tile(i):
        return pl.ds(pl.multiple_of(i * 8, 8), 8)

    def partial_copy(to, frm):
        return pltpu.make_async_remote_copy(
            src_ref=out2.at[tile(to)], dst_ref=partials_in.at[tile(frm)],
            send_sem=send2.at[to], recv_sem=recv2.at[frm],
            device_id=at(to, c), device_id_type=MESH,
        )

    def send_partial(i):
        partial_copy(lax.rem(q + 1 + i, slots), q).start()

    repeat(slots - 1, send_partial)
    partials_in[tile(q), :] = out2[tile(q), :]
    next_copy.wait_recv()

    def wait_partial(i):
        partial_copy(lax.rem(q + 1 + i, slots), lax.rem(q + 1 + i, slots)).wait_recv()

    repeat(slots - 1, wait_partial)
    valid = q * pairs + c < steps - 1

    def panel_step(r):
        def add(k, total):
            return total + jnp.where(
                row_ref[deal_ref[k]] == r, partials_in[pl.ds(pl.multiple_of(k * 8, 8), 8), :], 0.0)

        total = jnp.zeros((8, LANES), jnp.float32)
        if slots <= 32:
            for k in range(slots):
                total = add(k, total)
        else:
            total = lax.fori_loop(0, slots, add, total)
        predicted = jnp.tanh(total)
        target = following[r].astype(jnp.float32)
        mismatch = jnp.where(valid, predicted - target, 0.0)
        mismatches[tile(r), :] = mismatch
        gradients[r] = mismatch * (1.0 - predicted * predicted) * (1.0 / math.sqrt(steps))

    repeat(rows, panel_step)

    def pick_signal(k):
        out3[k] = gradients[row_ref[deal_ref[k]]].astype(jnp.bfloat16)

    repeat(slots, pick_signal)

    def signal_copy(to, frm):
        to_slot, to_core = lax.rem(to, slots), to // slots
        return pltpu.make_async_remote_copy(
            src_ref=out3.at[to_slot], dst_ref=signal_in.at[frm],
            send_sem=send3.at[to], recv_sem=recv3.at[frm],
            device_id=at(to_slot, to_core), device_id_type=MESH,
        )

    def send_signal(i):
        signal_copy(lax.rem(me + 1 + i, steps), me).start()

    repeat(steps - 1, send_signal)
    signal_in[me] = gradients[row_ref[deal_ref[q]]].astype(jnp.bfloat16)

    def gather_errors(i):
        lanes = pl.ds(i * LANES, LANES) if isinstance(i, int) else pl.ds(
            pl.multiple_of(i * LANES, LANES), LANES)
        errors_ref[:, lanes] = mismatches[pl.ds(i, 1), :].astype(jnp.bfloat16)

    repeat(rows * 8, gather_errors)
    pair_copy.wait_recv()
    work[...] = rates_in[...].astype(jnp.float32).reshape(steps * 8, LANES)
    for j in range(group):
        source_ref[:, j * LANES:(j + 1) * LANES] = work[pl.ds(j, steps, stride=8), :].astype(
            jnp.bfloat16)

    def drain(i):
        to = lax.rem(q + 1 + i, slots)
        rates_copy(to, q).wait_send()
        partial_copy(to, q).wait_send()

    repeat(slots - 1, drain)
    next_copy.wait_send()
    pair_copy.wait_send()

    def wait_signal(i):
        signal_copy(lax.rem(me + 1 + i, steps), lax.rem(me + 1 + i, steps)).wait_recv()

    repeat(steps - 1, wait_signal)
    work[...] = signal_in[...].astype(jnp.float32).reshape(steps * 8, LANES)
    half = group // pairs
    for j in range(half):
        signal_ref[:, j * LANES:(j + 1) * LANES] = work[
            pl.ds(c * half + j, steps, stride=8), :].astype(jnp.bfloat16)

    def drain_signal(i):
        signal_copy(lax.rem(me + 1 + i, steps), me).wait_send()

    repeat(steps - 1, drain_signal)


def gradient_kernel(signal_ref, source_ref, scale_ref, errors_ref, grads_ref, errors_out):
    term = lax.dot_general(
        signal_ref[...], source_ref[...], (((0,), (0,)), ((), ())),
        preferred_element_type=jnp.float32)
    grads_ref[0] = (term * scale_ref[...]).astype(jnp.bfloat16)
    errors_out[...] = errors_ref[...]


def shards(sizes, observed_rates, block_values, block_row, block_col, deal_list, scale_index,
           scale_table):
    regions, devs, pairs = sizes
    slots = regions * devs
    steps = slots * pairs
    neurons = observed_rates.shape[1]
    size = block_values.shape[1]
    rows = neurons // size
    bf16, f32 = jnp.bfloat16, jnp.float32
    vmem = pl.BlockSpec(memory_space=pltpu.VMEM)
    smem = pl.BlockSpec(memory_space=pltpu.SMEM)
    dma = pltpu.SemaphoreType.DMA
    signal, source, errors, scale = pl.pallas_call(
        functools.partial(exchange_kernel, regions, devs, pairs),
        out_shape=(
            jax.ShapeDtypeStruct((steps, size // pairs), bf16),
            jax.ShapeDtypeStruct((steps, size), bf16),
            jax.ShapeDtypeStruct((1, neurons), bf16),
            jax.ShapeDtypeStruct((1, size), f32),
        ),
        in_specs=[vmem, pl.BlockSpec(memory_space=pl.ANY)] + [smem] * 5,
        out_specs=(vmem,) * 4,
        scratch_shapes=[
            pltpu.VMEM((rows, 8, LANES), f32),
            pltpu.VMEM((rows, 8, LANES), bf16),
            pltpu.VMEM((rows, 8, LANES), bf16),
            pltpu.VMEM((slots, 8, LANES), bf16),
            pltpu.VMEM((steps, 8, LANES), bf16),
            pltpu.VMEM((size, size), bf16),
            pltpu.VMEM((steps * 8, LANES), f32),
            pltpu.VMEM((slots * 8, LANES), f32),
            pltpu.VMEM((slots * 8, LANES), f32),
            pltpu.VMEM((rows * 8, LANES), f32),
            pltpu.VMEM((rows, 8, LANES), f32),
            pltpu.VMEM((slots, 8, LANES), bf16),
            pltpu.VMEM((steps, 8, LANES), bf16),
            dma, dma((slots,)), dma((slots,)), dma, dma, dma, dma,
            dma((slots,)), dma((slots,)), dma((steps,)), dma((steps,)),
        ],
        compiler_params=pltpu.CompilerParams(
            collective_id=0, has_side_effects=True, vmem_limit_bytes=32 * 1024 * 1024),
        name="exchange",
    )(observed_rates, block_values, block_row, block_col, deal_list, scale_index, scale_table)
    grads, errors = pl.pallas_call(
        gradient_kernel,
        out_shape=(
            jax.ShapeDtypeStruct((1, size // pairs, size), bf16),
            jax.ShapeDtypeStruct((1, neurons), bf16),
        ),
        in_specs=[vmem] * 4,
        out_specs=(vmem, vmem),
        compiler_params=pltpu.CompilerParams(vmem_limit_bytes=32 * 1024 * 1024),
        name="gradient",
    )(signal, source, scale, errors)
    return (errors, grads)


def solution(mesh):
    sizes = (mesh.shape["region"], mesh.shape["dev"], mesh.shape["pair"])
    return jax.shard_map(
        functools.partial(shards, sizes),
        mesh=mesh,
        in_specs=(
            P(("parts", "region", "dev", "pair"), None),
            P(("parts", "region", "dev"), None, None),
            P("parts"),
            P("parts"),
            P("parts"),
            P(("parts", "region", "dev"), None),
            P("parts"),
        ),
        out_specs=(
            P(("parts", "region", "dev", "pair"), None),
            P(("parts", "region", "dev"), "pair", None),
        ),
        check_vma=False,
    )
```

time: 73.8 us -> 26.9 us (0.36)
  Pallas kernels: 0 us -> 20.3 us
  waiting for transfers between devices: 19.8 us -> 0 us
  between operations: 14.2 us -> 0.65 us
  starting transfers between devices: 12.6 us -> 0 us
  blocking collectives: 8.96 us -> 0 us
  other arithmetic: 7.47 us -> 0 us
  matrix products: 5.19 us -> 0 us
    pallas_call x0 -> x2, Pallas kernels: none -> 20.3 us  [the longest x1 18.9 us: shards(): pl.pallas_call(functools.partial(exchange_kernel, regions, devs, pairs),...]
    all_to_all x2 -> x0, starting transfers between devices: 11.2 us -> none  [the longest x1 7.88 us: shards(): lax.all_to_all(outgoing, ('region', 'dev'), split_axis=1, concat_axis=0,...]
    all_to_all x2 -> x0, waiting for transfers between devices: 10.9 us -> none  [the longest x1 6.6 us: shards(): lax.all_to_all(partial_value.reshape(blocks_all, step_dev, block), ('regi...]
    all_to_all x1 -> x0, blocking collectives: 8.96 us -> none  [shards(): lax.all_to_all(outgoing_signal, ('region', 'dev'), split_axis=1, concat_a...]
    reduce_scatter x1 -> x0, waiting for transfers between devices: 8.88 us -> none  [shards(): lax.psum_scatter(contract_time(arrived, source) * column_scale[None, :],...]
    dot_general x3 -> x0, matrix products: 5.19 us -> none  [the longest x1 2.68 us: contract_time(): lax.dot_general(signal_part, source_part, (((0,), (0,)), ((), ())), prefe...]
    unnamed x8 -> x14, local copies, waits for them, and re-layouts: 1.29 us -> 5.57 us
    gather x4 -> x0, local copies, waits for them, and re-layouts: 3.08 us -> none  [the longest x1 1.3 us: shards(): row_of = block_row[deal_list]]
  transfers between devices with their start and end apart: 4 -> 0, of which waited for: 3 -> 0; matrix products, arithmetic and copies ran while one was open for 15% -> 0% of each run, Pallas kernels for 0% -> 0%
where the time goes in v1:
time: 26.9 us; the launch traced here: 26.6 us
  Pallas kernels  20.3 us (75%)
  local copies, waits for them, and re-layouts  5.57 us (21%)
  between operations  0.65 us (2%)
    pallas_call x1, Pallas kernels, shards(): pl.pallas_call(functools.partial(exchange_kernel, regions, devs, pairs),...  18.9 us
    unnamed x14, local copies, waits for them, and re-layouts  5.57 us
    pallas_call x1, Pallas kernels, shards(): pl.pallas_call(gradient_kernel, out_shape=(jax.ShapeDtypeStruct((1, size...  1.43 us

profile of v1, /device:TPU:0, one launch (start us, length us, event | category | flops | bytes accessed | tf_op | source)
XLA Modules:
  0.0 26.6 jit_solution(9804528819280282891)
XLA Ops:
  0.6 0.0 copy-start
  0.6 1.6 %copy-done = bf16[1,1024,1024]{2,1,0:T(8,128)(2,1)S(1)} copy-done((bf16[1,1024,1024]{2,1,0:T(8,128)(2,1)S(1)}, bf16[1,1024,1024]{2,1,0:T(8,128)(2,1)}, u32[]{:S(2)}) %copy-start) | copy-done | bytes 2097176
  2.2 0.0 copy-start.1
  2.2 0.7 %copy-done.1 = bf16[1,4096]{1,0:T(2,128)(2,1)S(1)} copy-done((bf16[1,4096]{1,0:T(2,128)(2,1)S(1)}, bf16[1,4096]{1,0:T(2,128)(2,1)}, u32[]{:S(2)}) %copy-start.1) | copy-done | bytes 8216
  2.9 0.0 copy-start.2
  2.9 0.7 %copy-done.2 = s32[8]{0:T(128)S(1)} copy-done((s32[8]{0:T(128)S(1)}, s32[8]{0:T(128)}, u32[]{:S(2)}) %copy-start.2) | copy-done | bytes 56
  3.6 0.0 copy-start.3
  3.6 0.7 %copy-done.3 = s32[8]{0:T(128)S(1)} copy-done((s32[8]{0:T(128)S(1)}, s32[8]{0:T(128)}, u32[]{:S(2)}) %copy-start.3) | copy-done | bytes 56
  4.3 0.0 copy-start.4
  4.3 0.7 %copy-done.4 = s32[8]{0:T(128)S(1)} copy-done((s32[8]{0:T(128)S(1)}, s32[8]{0:T(128)}, u32[]{:S(2)}) %copy-start.4) | copy-done | bytes 56
  4.9 0.0 copy-start.5
  4.9 0.7 %copy-done.5 = s32[1,8]{1,0:T(1,128)S(1)} copy-done((s32[1,8]{1,0:T(1,128)S(1)}, s32[1,8]{1,0:T(1,128)}, u32[]{:S(2)}) %copy-start.5) | copy-done | bytes 56
  5.6 0.0 copy-start.6
  5.6 0.7 %copy-done.6 = f32[16]{0:T(128)S(1)} copy-done((f32[16]{0:T(128)S(1)}, f32[16]{0:T(128)}, u32[]{:S(2)}) %copy-start.6) | copy-done | bytes 88
  6.2 18.9 %exchange.1 = (bf16[16,512]{1,0:T(8,128)(2,1)S(1)}, bf16[16,1024]{1,0:T(8,128)(2,1)S(1)}, bf16[1,4096]{1,0:T(2,128)(2,1)S(1)}, f32[1,1024]{1,0:T(1,128)S(1)}) custom-call(bf16[1,4096]{1,0:T(2,128)(2,1)S(1)} %copy-done.1, bf16[1,1024,1024]{2,1,0:T(8,128)(2,1)S(1)} %copy-done, s32[8]{0:T(128)S(1)} %copy-done.2, s32[8]{0:T(128)S(1)} %copy-done.3, ...), custom_call_target="tpu_custom_call" | custom-call | tf_op jit(solution)/shard_map/exchange/pallas_call | solution.py:237
  25.1 1.4 %gradient.1 = (bf16[1,512,1024]{2,1,0:T(8,128)(2,1)}, bf16[1,4096]{1,0:T(2,128)(2,1)}) custom-call(bf16[16,512]{1,0:T(8,128)(2,1)S(1)} %get-tuple-element.8.signal_ref, bf16[16,1024]{1,0:T(8,128)(2,1)S(1)} %get-tuple-element.9.source_ref, f32[1,1024]{1,0:T(1,128)S(1)} %get-tuple-element.10.scale_ref, bf16[1,4096]{1,0:T(2,128)(2,1)S(1)} %get-tuple-element.11.errors_ref), custom_call_target="tpu_custom_call" | custom-call | tf_op jit(solution)/shard_map/gradient/pallas_call | solution.py:268
Async XLA Ops:
  0.6 1.6 %copy-start = (bf16[1,1024,1024]{2,1,0:T(8,128)(2,1)S(1)}, bf16[1,1024,1024]{2,1,0:T(8,128)(2,1)}, u32[]{:S(2)}) copy-start(bf16[1,1024,1024]{2,1,0:T(8,128)(2,1)} %values_ref.1) | copy-start | bytes 6291460
  2.2 0.7 %copy-start.1 = (bf16[1,4096]{1,0:T(2,128)(2,1)S(1)}, bf16[1,4096]{1,0:T(2,128)(2,1)}, u32[]{:S(2)}) copy-start(bf16[1,4096]{1,0:T(2,128)(2,1)} %rates_ref.1) | copy-start | bytes 24580
  2.9 0.7 %copy-start.2 = (s32[8]{0:T(128)S(1)}, s32[8]{0:T(128)}, u32[]{:S(2)}) copy-start(s32[8]{0:T(128)} %row_ref.1) | copy-start | bytes 100
  3.6 0.7 %copy-start.3 = (s32[8]{0:T(128)S(1)}, s32[8]{0:T(128)}, u32[]{:S(2)}) copy-start(s32[8]{0:T(128)} %col_ref.1) | copy-start | bytes 100
  4.3 0.7 %copy-start.4 = (s32[8]{0:T(128)S(1)}, s32[8]{0:T(128)}, u32[]{:S(2)}) copy-start(s32[8]{0:T(128)} %deal_ref.1) | copy-start | bytes 100
  4.9 0.7 %copy-start.5 = (s32[1,8]{1,0:T(1,128)S(1)}, s32[1,8]{1,0:T(1,128)}, u32[]{:S(2)}) copy-start(s32[1,8]{1,0:T(1,128)} %index_ref.1) | copy-start | bytes 100
  5.6 0.7 %copy-start.6 = (f32[16]{0:T(128)S(1)}, f32[16]{0:T(128)}, u32[]{:S(2)}) copy-start(f32[16]{0:T(128)} %table_ref.1) | copy-start | bytes 196

commit v2 on v1

--- a/solution.py
+++ b/solution.py
@@ -22,10 +22,11 @@
 
 def exchange_kernel(
     regions, devs, pairs,
-    rates_ref, values_ref, row_ref, col_ref, deal_ref, index_ref, table_ref,
+    rates_hbm, values_hbm, row_hbm, col_hbm, deal_hbm, index_hbm, table_hbm,
     signal_ref, source_ref, errors_ref, scale_ref,
     panels, panels16, following, out1, rates_in, block, work, out2, partials_in,
     mismatches, gradients, out3, signal_in,
+    rates_ref, row_ref, col_ref, deal_ref, index_ref, table_ref, small_sem,
     block_sem, send1, recv1, send_next, recv_next, send_pair, recv_pair,
     send2, recv2, send3, recv3,
 ):
@@ -41,7 +42,15 @@
     def at(slot, core):
         return {"region": slot // devs, "dev": slot % devs, "pair": core}
 
-    load = pltpu.make_async_copy(values_ref.at[0], block, block_sem)
+    smalls = [
+        pltpu.make_async_copy(source, held, small_sem.at[i])
+        for i, (source, held) in enumerate((
+            (rates_hbm, rates_ref), (col_hbm, col_ref), (deal_hbm, deal_ref),
+            (row_hbm, row_ref), (index_hbm, index_ref), (table_hbm, table_ref)))
+    ]
+    for copy in smalls:
+        copy.start()
+    load = pltpu.make_async_copy(values_hbm.at[0], block, block_sem)
     load.start()
 
     barrier = pltpu.get_barrier_semaphore()
@@ -53,6 +62,9 @@
         )
 
     repeat(steps - 1, greet)
+
+    for copy in smalls:
+        copy.wait()
 
     def spread(i):
         lanes = pl.ds(i * LANES, LANES) if isinstance(i, int) else pl.ds(
@@ -232,7 +244,6 @@
     rows = neurons // size
     bf16, f32 = jnp.bfloat16, jnp.float32
     vmem = pl.BlockSpec(memory_space=pltpu.VMEM)
-    smem = pl.BlockSpec(memory_space=pltpu.SMEM)
     dma = pltpu.SemaphoreType.DMA
     signal, source, errors, scale = pl.pallas_call(
         functools.partial(exchange_kernel, regions, devs, pairs),
@@ -242,7 +253,7 @@
             jax.ShapeDtypeStruct((1, neurons), bf16),
             jax.ShapeDtypeStruct((1, size), f32),
         ),
-        in_specs=[vmem, pl.BlockSpec(memory_space=pl.ANY)] + [smem] * 5,
+        in_specs=[pl.BlockSpec(memory_space=pltpu.HBM)] * 7,
         out_specs=(vmem,) * 4,
         scratch_shapes=[
             pltpu.VMEM((rows, 8, LANES), f32),
@@ -258,13 +269,21 @@
             pltpu.VMEM((rows, 8, LANES), f32),
             pltpu.VMEM((slots, 8, LANES), bf16),
             pltpu.VMEM((steps, 8, LANES), bf16),
+            pltpu.VMEM((1, neurons), bf16),
+            pltpu.SMEM(block_row.shape, jnp.int32),
+            pltpu.SMEM(block_col.shape, jnp.int32),
+            pltpu.SMEM(deal_list.shape, jnp.int32),
+            pltpu.SMEM(scale_index.shape, jnp.int32),
+            pltpu.SMEM(scale_table.shape, f32),
+            dma((6,)),
             dma, dma((slots,)), dma((slots,)), dma, dma, dma, dma,
             dma((slots,)), dma((slots,)), dma((steps,)), dma((steps,)),
         ],
         compiler_params=pltpu.CompilerParams(
             collective_id=0, has_side_effects=True, vmem_limit_bytes=32 * 1024 * 1024),
         name="exchange",
-    )(observed_rates, block_values, block_row, block_col, deal_list, scale_index, scale_table)
+    )(*(pltpu.with_memory_space_constraint(operand, pltpu.HBM) for operand in (
+        observed_rates, block_values, block_row, block_col, deal_list, scale_index, scale_table)))
     grads, errors = pl.pallas_call(
         gradient_kernel,
         out_shape=(

time: 26.9 us -> 20.6 us (0.77)
  local copies, waits for them, and re-layouts: 5.57 us -> 0 us
  Pallas kernels: 20.3 us -> 19.7 us
    unnamed x14 -> x0, local copies, waits for them, and re-layouts: 5.57 us -> none
    pallas_call x1, Pallas kernels: 18.9 us -> 18.3 us  [shards(): pl.pallas_call(functools.partial(exchange_kernel, regions, devs, pairs),...]
where the time goes in v2:
time: 20.6 us; the launch traced here: 20.3 us
  Pallas kernels  19.7 us (96%)
  between operations  0.64 us (3%)
    pallas_call x1, Pallas kernels, shards(): pl.pallas_call(functools.partial(exchange_kernel, regions, devs, pairs),...  18.3 us
    pallas_call x1, Pallas kernels, shards(): pl.pallas_call(gradient_kernel, out_shape=(jax.ShapeDtypeStruct((1, size...  1.43 us

profile of v2, /device:TPU:0, one launch (start us, length us, event | category | flops | bytes accessed | tf_op | source)
XLA Modules:
  0.0 20.3 jit_solution(3012373306493648705)
XLA Ops:
  0.6 18.3 %exchange.1 = (bf16[16,512]{1,0:T(8,128)(2,1)S(1)}, bf16[16,1024]{1,0:T(8,128)(2,1)S(1)}, bf16[1,4096]{1,0:T(2,128)(2,1)S(1)}, f32[1,1024]{1,0:T(1,128)S(1)}) custom-call(bf16[1,4096]{1,0:T(2,128)(2,1)} %rates_hbm.1, bf16[1,1024,1024]{2,1,0:T(8,128)(2,1)} %values_hbm.1, s32[8]{0:T(128)} %row_hbm.1, s32[8]{0:T(128)} %col_hbm.1, s32[8]{0:T(128)} %deal_hbm.1, ...), custom_call_target="tpu_custom_call" | custom-call | tf_op jit(solution)/shard_map/exchange/pallas_call | solution.py:248
  18.9 1.4 %gradient.1 = (bf16[1,512,1024]{2,1,0:T(8,128)(2,1)}, bf16[1,4096]{1,0:T(2,128)(2,1)}) custom-call(bf16[16,512]{1,0:T(8,128)(2,1)S(1)} %get-tuple-element.8.signal_ref, bf16[16,1024]{1,0:T(8,128)(2,1)S(1)} %get-tuple-element.9.source_ref, f32[1,1024]{1,0:T(1,128)S(1)} %get-tuple-element.10.scale_ref, bf16[1,4096]{1,0:T(2,128)(2,1)S(1)} %get-tuple-element.11.errors_ref), custom_call_target="tpu_custom_call" | custom-call | tf_op jit(solution)/shard_map/gradient/pallas_call | solution.py:287

commit v3 on v2

v3 whole, which is shorter than its diff:
```python
import functools
import math

import jax
import jax.numpy as jnp
from jax import lax
from jax.experimental import pallas as pl
from jax.experimental.pallas import tpu as pltpu
from jax.sharding import PartitionSpec as P

LANES = 128
MESH = pl.DeviceIdType.MESH


def repeat(count, body):
    if count <= 32:
        for i in range(count):
            body(i)
    else:
        lax.fori_loop(0, count, lambda i, carry: (body(i), carry)[1], 0)


def exchange_kernel(
    regions, devs, pairs,
    rates_hbm, values_hbm, row_hbm, col_hbm, deal_hbm, index_hbm, table_hbm,
    signal_ref, source_ref, errors_ref, scale_ref,
    panels, panels16, following, out1, rates_in, block, work, halves, halves_in, out2, partials_in,
    mismatches,
    rates_ref, row_ref, col_ref, deal_ref, index_ref, table_ref, small_sem,
    block_sem, send1, recv1, send_next, recv_next, send2, recv2, send3, recv3,
):
    slots = regions * devs
    steps = slots * pairs
    rows = panels.shape[0]
    half = block.shape[0]
    group = block.shape[1] // LANES
    part = half // LANES
    c = lax.axis_index("pair")
    q = lax.axis_index("region") * devs + lax.axis_index("dev")
    me = q * pairs + c

    def at(slot, core):
        return {"region": slot // devs, "dev": slot % devs, "pair": core}

    def at_step(step):
        return at(step // pairs, lax.rem(step, pairs))

    def other_step(i):
        return lax.rem(me + 1 + i, steps)

    def other_slot(i):
        return lax.rem(q + 1 + i, slots)

    def tile(i):
        return pl.ds(pl.multiple_of(i * 8, 8), 8)

    def lanes_of(i):
        return pl.ds(i * LANES, LANES) if isinstance(i, int) else pl.ds(
            pl.multiple_of(i * LANES, LANES), LANES)

    smalls = [
        pltpu.make_async_copy(source, held, small_sem.at[i])
        for i, (source, held) in enumerate((
            (rates_hbm, rates_ref), (col_hbm, col_ref), (deal_hbm, deal_ref),
            (row_hbm, row_ref), (index_hbm, index_ref), (table_hbm, table_ref)))
    ]
    for copy in smalls:
        copy.start()
    load = pltpu.make_async_copy(
        values_hbm.at[0, pl.ds(pl.multiple_of(c * half, half), half)], block, block_sem)
    load.start()

    barrier = pltpu.get_barrier_semaphore()

    def greet(i):
        pl.semaphore_signal(
            barrier, inc=1, device_id=at_step(other_step(i)), device_id_type=MESH)

    repeat(steps - 1, greet)
    for copy in smalls:
        copy.wait()

    def spread(i):
        panels[i // 8, pl.ds(i % 8, 1), :] = rates_ref[:, lanes_of(i)].astype(jnp.float32)

    repeat(rows * 8, spread)
    panels16[...] = panels[...].astype(jnp.bfloat16)

    def pick(k):
        out1[k, 0] = panels[col_ref[deal_ref[k]]].astype(jnp.bfloat16)
        out1[k, 1] = panels[row_ref[deal_ref[k]]].astype(jnp.bfloat16)

    repeat(slots, pick)
    my_row = row_ref[deal_ref[q]]
    rates_in[me, 0] = panels[col_ref[deal_ref[q]]].astype(jnp.bfloat16)
    rates_in[me, 1] = panels[my_row].astype(jnp.bfloat16)
    rates_in[steps] = jnp.zeros(rates_in.shape[1:], jnp.bfloat16)
    pl.semaphore_wait(barrier, steps - 1)

    def rates_copy(to, frm):
        return pltpu.make_async_remote_copy(
            src_ref=out1.at[to // pairs], dst_ref=rates_in.at[frm],
            send_sem=send1.at[to], recv_sem=recv1.at[frm],
            device_id=at_step(to), device_id_type=MESH,
        )

    repeat(steps - 1, lambda i: rates_copy(other_step(i), me).start())
    next_copy = pltpu.make_async_remote_copy(
        src_ref=panels16, dst_ref=following, send_sem=send_next, recv_sem=recv_next,
        device_id=at_step(lax.rem(me + steps - 1, steps)), device_id_type=MESH,
    )
    next_copy.start()

    for g in range(group):
        scale_ref[:, g * LANES:(g + 1) * LANES] = jnp.full(
            (1, LANES), table_ref[index_ref[0, g]], jnp.float32)

    def same_row(k, found):
        return jnp.maximum(found, jnp.where((row_ref[deal_ref[k]] == my_row) & (k != q), k, 0))

    partner = jnp.int32(0)
    if slots <= 32:
        for k in range(slots):
            partner = same_row(k, partner)
    else:
        partner = lax.fori_loop(0, slots, same_row, partner)
    load.wait()
    chunk = 64

    @pl.loop(0, half // chunk)
    def _(i):
        piece = pl.ds(pl.multiple_of(i * chunk, chunk), chunk)
        block[piece, :] = (block[piece, :].astype(jnp.float32) * scale_ref[...]).astype(
            jnp.bfloat16)

    repeat(steps - 1, lambda i: rates_copy(other_step(i), other_step(i)).wait_recv())
    work[...] = rates_in[pl.ds(0, steps), 0].astype(jnp.float32).reshape(steps * 8, LANES)
    for j in range(group):
        source_ref[:, j * LANES:(j + 1) * LANES] = work[pl.ds(j, steps, stride=8), :].astype(
            jnp.bfloat16)
    partial_value = lax.dot_general(
        source_ref[...], block[...], (((1,), (1,)), ((), ())), preferred_element_type=jnp.float32)
    halves[...] = partial_value.astype(jnp.bfloat16)
    halves_in[q] = halves[...]

    def half_copy(to, frm):
        return pltpu.make_async_remote_copy(
            src_ref=halves, dst_ref=halves_in.at[frm],
            send_sem=send2.at[to], recv_sem=recv2.at[frm],
            device_id=at(to, c), device_id_type=MESH,
        )

    repeat(slots - 1, lambda i: half_copy(other_slot(i), q).start())
    for j in range(8):
        k = j % part
        out2[pl.ds(j, steps, stride=8), :] = partial_value[:, k * LANES:(k + 1) * LANES]

    def partial_copy(to, frm):
        return pltpu.make_async_remote_copy(
            src_ref=out2.at[tile(to)], dst_ref=partials_in.at[tile(frm)],
            send_sem=send3.at[to], recv_sem=recv3.at[frm],
            device_id=at_step(to), device_id_type=MESH,
        )

    repeat(steps - 1, lambda i: partial_copy(other_step(i), me).start())
    partials_in[tile(me), :] = out2[tile(me), :]
    work[...] = rates_in[pl.ds(1, steps), 1].astype(jnp.float32).reshape(steps * 8, LANES)
    target = jnp.concatenate(
        [work[pl.ds(c * part + j, steps, stride=8), :] for j in range(part)], axis=1)
    row = lax.broadcasted_iota(jnp.int32, (steps, half), 0)
    repeat(steps - 1, lambda i: rates_copy(other_step(i), me).wait_send())
    next_copy.wait()

    repeat(slots - 1, lambda i: half_copy(other_slot(i), other_slot(i)).wait_recv())
    scale = 1.0 / math.sqrt(steps)
    predicted = jnp.tanh(partial_value + halves_in[partner].astype(jnp.float32))
    mismatch = jnp.where(row < steps - 1, predicted - target, 0.0)
    signal_ref[...] = (mismatch * (1.0 - predicted * predicted) * scale).astype(jnp.bfloat16)

    repeat(steps - 1, lambda i: partial_copy(other_step(i), other_step(i)).wait_recv())

    def panel_step(r):
        def add(k, total):
            value = jnp.concatenate(
                [partials_in[tile(k * pairs + core), :][:part] for core in range(pairs)], axis=0)
            return total + jnp.where(row_ref[deal_ref[k]] == r, value, 0.0)

        total = jnp.zeros((8, LANES), jnp.float32)
        if slots <= 32:
            for k in range(slots):
                total = add(k, total)
        else:
            total = lax.fori_loop(0, slots, add, total)
        mismatches[tile(r), :] = jnp.where(
            me < steps - 1, jnp.tanh(total) - following[r].astype(jnp.float32), 0.0)

    repeat(rows, panel_step)

    def gather_errors(i):
        errors_ref[:, lanes_of(i)] = mismatches[pl.ds(i, 1), :].astype(jnp.bfloat16)

    repeat(rows * 8, gather_errors)
    repeat(slots - 1, lambda i: half_copy(other_slot(i), q).wait_send())
    repeat(steps - 1, lambda i: partial_copy(other_step(i), me).wait_send())


def gradient_kernel(signal_ref, source_ref, scale_ref, errors_ref, grads_ref, errors_out):
    term = lax.dot_general(
        signal_ref[...], source_ref[...], (((0,), (0,)), ((), ())),
        preferred_element_type=jnp.float32)
    grads_ref[0] = (term * scale_ref[...]).astype(jnp.bfloat16)
    errors_out[...] = errors_ref[...]


def shards(sizes, observed_rates, block_values, block_row, block_col, deal_list, scale_index,
           scale_table):
    regions, devs, pairs = sizes
    slots = regions * devs
    steps = slots * pairs
    neurons = observed_rates.shape[1]
    size = block_values.shape[1]
    rows = neurons // size
    bf16, f32 = jnp.bfloat16, jnp.float32
    vmem = pl.BlockSpec(memory_space=pltpu.VMEM)
    dma = pltpu.SemaphoreType.DMA
    signal, source, errors, scale = pl.pallas_call(
        functools.partial(exchange_kernel, regions, devs, pairs),
        out_shape=(
            jax.ShapeDtypeStruct((steps, size // pairs), bf16),
            jax.ShapeDtypeStruct((steps, size), bf16),
            jax.ShapeDtypeStruct((1, neurons), bf16),
            jax.ShapeDtypeStruct((1, size), f32),
        ),
        in_specs=[pl.BlockSpec(memory_space=pltpu.HBM)] * 7,
        out_specs=(vmem,) * 4,
        scratch_shapes=[
            pltpu.VMEM((rows, 8, LANES), f32),
            pltpu.VMEM((rows, 8, LANES), bf16),
            pltpu.VMEM((rows, 8, LANES), bf16),
            pltpu.VMEM((slots, 2, 8, LANES), bf16),
            pltpu.VMEM((steps + 1, 2, 8, LANES), bf16),
            pltpu.VMEM((size // pairs, size), bf16),
            pltpu.VMEM((steps * 8, LANES), f32),
            pltpu.VMEM((steps, size // pairs), bf16),
            pltpu.VMEM((slots, steps, size // pairs), bf16),
            pltpu.VMEM((steps * 8, LANES), f32),
            pltpu.VMEM((steps * 8, LANES), f32),
            pltpu.VMEM((rows * 8, LANES), f32),
            pltpu.VMEM((1, neurons), bf16),
            pltpu.SMEM(block_row.shape, jnp.int32),
            pltpu.SMEM(block_col.shape, jnp.int32),
            pltpu.SMEM(deal_list.shape, jnp.int32),
            pltpu.SMEM(scale_index.shape, jnp.int32),
            pltpu.SMEM(scale_table.shape, f32),
            dma((6,)),
            dma, dma((steps,)), dma((steps,)), dma, dma,
            dma((slots,)), dma((slots,)), dma((steps,)), dma((steps,)),
        ],
        compiler_params=pltpu.CompilerParams(
            collective_id=0, has_side_effects=True, vmem_limit_bytes=48 * 1024 * 1024),
        name="exchange",
    )(*(pltpu.with_memory_space_constraint(operand, pltpu.HBM) for operand in (
        observed_rates, block_values, block_row, block_col, deal_list, scale_index, scale_table)))
    grads, errors = pl.pallas_call(
        gradient_kernel,
        out_shape=(
            jax.ShapeDtypeStruct((1, size // pairs, size), bf16),
            jax.ShapeDtypeStruct((1, neurons), bf16),
        ),
        in_specs=[vmem] * 4,
        out_specs=(vmem, vmem),
        compiler_params=pltpu.CompilerParams(vmem_limit_bytes=32 * 1024 * 1024),
        name="gradient",
    )(signal, source, scale, errors)
    return (errors, grads)


def solution(mesh):
    sizes = (mesh.shape["region"], mesh.shape["dev"], mesh.shape["pair"])
    return jax.shard_map(
        functools.partial(shards, sizes),
        mesh=mesh,
        in_specs=(
            P(("parts", "region", "dev", "pair"), None),
            P(("parts", "region", "dev"), None, None),
            P("parts"),
            P("parts"),
            P("parts"),
            P(("parts", "region", "dev"), None),
            P("parts"),
        ),
        out_specs=(
            P(("parts", "region", "dev", "pair"), None),
            P(("parts", "region", "dev"), "pair", None),
        ),
        check_vma=False,
    )
```

time: 20.6 us -> 20.1 us (0.976)
  Pallas kernels: 19.7 us -> 19.2 us
    pallas_call x1, Pallas kernels: 18.3 us -> 17.8 us  [shards(): pl.pallas_call(functools.partial(exchange_kernel, regions, devs, pairs),...]
where the time goes in v3:
time: 20.1 us; the launch traced here: 19.8 us
  Pallas kernels  19.2 us (96%)
  between operations  0.64 us (3%)
    pallas_call x1, Pallas kernels, shards(): pl.pallas_call(functools.partial(exchange_kernel, regions, devs, pairs),...  17.8 us
    pallas_call x1, Pallas kernels, shards(): pl.pallas_call(gradient_kernel, out_shape=(jax.ShapeDtypeStruct((1, size...  1.43 us

profile of v3, /device:TPU:0, one launch (start us, length us, event | category | flops | bytes accessed | tf_op | source)
XLA Modules:
  0.0 19.8 jit_solution(7307212621046900752)
XLA Ops:
  0.6 17.8 %exchange.1 = (bf16[16,512]{1,0:T(8,128)(2,1)S(1)}, bf16[16,1024]{1,0:T(8,128)(2,1)S(1)}, bf16[1,4096]{1,0:T(2,128)(2,1)S(1)}, f32[1,1024]{1,0:T(1,128)S(1)}) custom-call(bf16[1,4096]{1,0:T(2,128)(2,1)} %rates_hbm.1, bf16[1,1024,1024]{2,1,0:T(8,128)(2,1)} %values_hbm.1, s32[8]{0:T(128)} %row_hbm.1, s32[8]{0:T(128)} %col_hbm.1, s32[8]{0:T(128)} %deal_hbm.1, ...), custom_call_target="tpu_custom_call" | custom-call | tf_op jit(solution)/shard_map/exchange/pallas_call | solution.py:226
  18.4 1.4 %gradient.1 = (bf16[1,512,1024]{2,1,0:T(8,128)(2,1)}, bf16[1,4096]{1,0:T(2,128)(2,1)}) custom-call(bf16[16,512]{1,0:T(8,128)(2,1)S(1)} %get-tuple-element.8.signal_ref, bf16[16,1024]{1,0:T(8,128)(2,1)S(1)} %get-tuple-element.9.source_ref, f32[1,1024]{1,0:T(1,128)S(1)} %get-tuple-element.10.scale_ref, bf16[1,4096]{1,0:T(2,128)(2,1)S(1)} %get-tuple-element.11.errors_ref), custom_call_target="tpu_custom_call" | custom-call | tf_op jit(solution)/shard_map/gradient/pallas_call | solution.py:264

commit v4 on v3

--- a/solution.py
+++ b/solution.py
@@ -24,8 +24,8 @@
     regions, devs, pairs,
     rates_hbm, values_hbm, row_hbm, col_hbm, deal_hbm, index_hbm, table_hbm,
     signal_ref, source_ref, errors_ref, scale_ref,
-    panels, panels16, following, out1, rates_in, block, work, halves, halves_in, out2, partials_in,
-    mismatches,
+    panels, panels16, following, out1, rates_in, block, work, halves, halves_in, sums,
+    target_row,
     rates_ref, row_ref, col_ref, deal_ref, index_ref, table_ref, small_sem,
     block_sem, send1, recv1, send_next, recv_next, send2, recv2, send3, recv3,
 ):
@@ -51,9 +51,6 @@
     def other_slot(i):
         return lax.rem(q + 1 + i, slots)
 
-    def tile(i):
-        return pl.ds(pl.multiple_of(i * 8, 8), 8)
-
     def lanes_of(i):
         return pl.ds(i * LANES, LANES) if isinstance(i, int) else pl.ds(
             pl.multiple_of(i * LANES, LANES), LANES)
@@ -151,19 +148,6 @@
         )
 
     repeat(slots - 1, lambda i: half_copy(other_slot(i), q).start())
-    for j in range(8):
-        k = j % part
-        out2[pl.ds(j, steps, stride=8), :] = partial_value[:, k * LANES:(k + 1) * LANES]
-
-    def partial_copy(to, frm):
-        return pltpu.make_async_remote_copy(
-            src_ref=out2.at[tile(to)], dst_ref=partials_in.at[tile(frm)],
-            send_sem=send3.at[to], recv_sem=recv3.at[frm],
-            device_id=at_step(to), device_id_type=MESH,
-        )
-
-    repeat(steps - 1, lambda i: partial_copy(other_step(i), me).start())
-    partials_in[tile(me), :] = out2[tile(me), :]
     work[...] = rates_in[pl.ds(1, steps), 1].astype(jnp.float32).reshape(steps * 8, LANES)
     target = jnp.concatenate(
         [work[pl.ds(c * part + j, steps, stride=8), :] for j in range(part)], axis=1)
@@ -171,37 +155,58 @@
     repeat(steps - 1, lambda i: rates_copy(other_step(i), me).wait_send())
     next_copy.wait()
 
+    panels[...] = following[...].astype(jnp.float32)
+
+    def lay_out(i):
+        target_row[:, lanes_of(i)] = panels[i // 8, pl.ds(i % 8, 1), :]
+
+    repeat(rows * 8, lay_out)
+    line = lax.broadcasted_iota(jnp.int32, (rows * pairs, steps), 0)
+    step = lax.broadcasted_iota(jnp.int32, (rows * pairs, steps), 1)
+    held_step = step == q * pairs + line // rows
+
+    def chosen(k):
+        hit = held_step & (lax.rem(line, rows) == row_ref[deal_ref[k]])
+        return jnp.where(hit, 1.0, 0.0)
+
+    few = slots * steps <= 512
+    if few:
+        choice = jnp.concatenate([chosen(k) for k in range(slots)], axis=1).astype(jnp.bfloat16)
     repeat(slots - 1, lambda i: half_copy(other_slot(i), other_slot(i)).wait_recv())
+
+    if few:
+        sums[0] = jnp.dot(choice, halves_in[...].reshape(slots * steps, half),
+                          preferred_element_type=jnp.float32)
+    else:
+        sums[0] = jnp.zeros(sums.shape[1:], jnp.float32)
+
+        @pl.loop(0, slots)
+        def _(k):
+            sums[0] = sums[0] + jnp.dot(
+                chosen(k).astype(jnp.bfloat16), halves_in[k], preferred_element_type=jnp.float32)
+
+    sum_copy = pltpu.make_async_remote_copy(
+        src_ref=sums.at[0], dst_ref=sums.at[1], send_sem=send3, recv_sem=recv3,
+        device_id=at(q, 1 - c), device_id_type=MESH,
+    )
+    sum_copy.start()
     scale = 1.0 / math.sqrt(steps)
     predicted = jnp.tanh(partial_value + halves_in[partner].astype(jnp.float32))
     mismatch = jnp.where(row < steps - 1, predicted - target, 0.0)
     signal_ref[...] = (mismatch * (1.0 - predicted * predicted) * scale).astype(jnp.bfloat16)
 
-    repeat(steps - 1, lambda i: partial_copy(other_step(i), other_step(i)).wait_recv())
-
-    def panel_step(r):
-        def add(k, total):
-            value = jnp.concatenate(
-                [partials_in[tile(k * pairs + core), :][:part] for core in range(pairs)], axis=0)
-            return total + jnp.where(row_ref[deal_ref[k]] == r, value, 0.0)
-
-        total = jnp.zeros((8, LANES), jnp.float32)
-        if slots <= 32:
-            for k in range(slots):
-                total = add(k, total)
-        else:
-            total = lax.fori_loop(0, slots, add, total)
-        mismatches[tile(r), :] = jnp.where(
-            me < steps - 1, jnp.tanh(total) - following[r].astype(jnp.float32), 0.0)
-
-    repeat(rows, panel_step)
-
-    def gather_errors(i):
-        errors_ref[:, lanes_of(i)] = mismatches[pl.ds(i, 1), :].astype(jnp.bfloat16)
-
-    repeat(rows * 8, gather_errors)
     repeat(slots - 1, lambda i: half_copy(other_slot(i), q).wait_send())
-    repeat(steps - 1, lambda i: partial_copy(other_step(i), me).wait_send())
+    sum_copy.wait()
+    mine, theirs = sums[0], sums[1]
+    first = c == 0
+    mine = jnp.where(first, mine[:rows], mine[rows:])
+    theirs = jnp.where(first, theirs[:rows], theirs[rows:])
+    predicted = jnp.tanh(jnp.concatenate(
+        [jnp.where(first, mine, theirs), jnp.where(first, theirs, mine)], axis=1))
+    for r in range(rows):
+        lanes = slice(r * pairs * half, (r + 1) * pairs * half)
+        errors_ref[:, lanes] = jnp.where(
+            me < steps - 1, predicted[r:r + 1] - target_row[:, lanes], 0.0).astype(jnp.bfloat16)
 
 
 def gradient_kernel(signal_ref, source_ref, scale_ref, errors_ref, grads_ref, errors_out):
@@ -243,9 +248,8 @@
             pltpu.VMEM((steps * 8, LANES), f32),
             pltpu.VMEM((steps, size // pairs), bf16),
             pltpu.VMEM((slots, steps, size // pairs), bf16),
-            pltpu.VMEM((steps * 8, LANES), f32),
-            pltpu.VMEM((steps * 8, LANES), f32),
-            pltpu.VMEM((rows * 8, LANES), f32),
+            pltpu.VMEM((2, rows * pairs, size // pairs), f32),
+            pltpu.VMEM((1, neurons), f32),
             pltpu.VMEM((1, neurons), bf16),
             pltpu.SMEM(block_row.shape, jnp.int32),
             pltpu.SMEM(block_col.shape, jnp.int32),
@@ -254,7 +258,7 @@
             pltpu.SMEM(scale_table.shape, f32),
             dma((6,)),
             dma, dma((steps,)), dma((steps,)), dma, dma,
-            dma((slots,)), dma((slots,)), dma((steps,)), dma((steps,)),
+            dma((slots,)), dma((slots,)), dma, dma,
         ],
         compiler_params=pltpu.CompilerParams(
             collective_id=0, has_side_effects=True, vmem_limit_bytes=48 * 1024 * 1024),

time: 20.1 us -> 19.1 us (0.950)
  Pallas kernels: 19.2 us -> 18.2 us
    pallas_call x1, Pallas kernels: 17.8 us -> 16.8 us  [shards(): pl.pallas_call(functools.partial(exchange_kernel, regions, devs, pairs),...]
where the time goes in v4:
time: 19.1 us; the launch traced here: 18.8 us
  Pallas kernels  18.2 us (95%)
  between operations  0.64 us (3%)
    pallas_call x1, Pallas kernels, shards(): pl.pallas_call(functools.partial(exchange_kernel, regions, devs, pairs),...  16.8 us
    pallas_call x1, Pallas kernels, shards(): pl.pallas_call(gradient_kernel, out_shape=(jax.ShapeDtypeStruct((1, size...  1.43 us

profile of v4, /device:TPU:0, one launch (start us, length us, event | category | flops | bytes accessed | tf_op | source)
XLA Modules:
  0.0 18.8 jit_solution(16345943629768934928)
XLA Ops:
  0.6 16.8 %exchange.1 = (bf16[16,512]{1,0:T(8,128)(2,1)S(1)}, bf16[16,1024]{1,0:T(8,128)(2,1)S(1)}, bf16[1,4096]{1,0:T(2,128)(2,1)S(1)}, f32[1,1024]{1,0:T(1,128)S(1)}) custom-call(bf16[1,4096]{1,0:T(2,128)(2,1)} %rates_hbm.1, bf16[1,1024,1024]{2,1,0:T(8,128)(2,1)} %values_hbm.1, s32[8]{0:T(128)} %row_hbm.1, s32[8]{0:T(128)} %col_hbm.1, s32[8]{0:T(128)} %deal_hbm.1, ...), custom_call_target="tpu_custom_call" | custom-call | tf_op jit(solution)/shard_map/exchange/pallas_call | solution.py:231
  17.4 1.4 %gradient.1 = (bf16[1,512,1024]{2,1,0:T(8,128)(2,1)}, bf16[1,4096]{1,0:T(2,128)(2,1)}) custom-call(bf16[16,512]{1,0:T(8,128)(2,1)S(1)} %get-tuple-element.8.signal_ref, bf16[16,1024]{1,0:T(8,128)(2,1)S(1)} %get-tuple-element.9.source_ref, f32[1,1024]{1,0:T(1,128)S(1)} %get-tuple-element.10.scale_ref, bf16[1,4096]{1,0:T(2,128)(2,1)S(1)} %get-tuple-element.11.errors_ref), custom_call_target="tpu_custom_call" | custom-call | tf_op jit(solution)/shard_map/gradient/pallas_call | solution.py:268

commit v5 on v4

--- a/solution.py
+++ b/solution.py
@@ -138,7 +138,6 @@
     partial_value = lax.dot_general(
         source_ref[...], block[...], (((1,), (1,)), ((), ())), preferred_element_type=jnp.float32)
     halves[...] = partial_value.astype(jnp.bfloat16)
-    halves_in[q] = halves[...]
 
     def half_copy(to, frm):
         return pltpu.make_async_remote_copy(
@@ -148,6 +147,7 @@
         )
 
     repeat(slots - 1, lambda i: half_copy(other_slot(i), q).start())
+    halves_in[q] = halves[...]
     work[...] = rates_in[pl.ds(1, steps), 1].astype(jnp.float32).reshape(steps * 8, LANES)
     target = jnp.concatenate(
         [work[pl.ds(c * part + j, steps, stride=8), :] for j in range(part)], axis=1)

time: 19.1 us -> 19.1 us (level)
  no operation moved by 1% of the time
where the time goes in v5:
time: 19.1 us; the launch traced here: 18.8 us
  Pallas kernels  18.2 us (95%)
  between operations  0.64 us (3%)
    pallas_call x1, Pallas kernels, shards(): pl.pallas_call(functools.partial(exchange_kernel, regions, devs, pairs),...  16.8 us
    pallas_call x1, Pallas kernels, shards(): pl.pallas_call(gradient_kernel, out_shape=(jax.ShapeDtypeStruct((1, size...  1.43 us

profile of v5, /device:TPU:0, one launch (start us, length us, event | category | flops | bytes accessed | tf_op | source)
XLA Modules:
  0.0 18.8 jit_solution(295206242944269422)
XLA Ops:
  0.6 16.8 %exchange.1 = (bf16[16,512]{1,0:T(8,128)(2,1)S(1)}, bf16[16,1024]{1,0:T(8,128)(2,1)S(1)}, bf16[1,4096]{1,0:T(2,128)(2,1)S(1)}, f32[1,1024]{1,0:T(1,128)S(1)}) custom-call(bf16[1,4096]{1,0:T(2,128)(2,1)} %rates_hbm.1, bf16[1,1024,1024]{2,1,0:T(8,128)(2,1)} %values_hbm.1, s32[8]{0:T(128)} %row_hbm.1, s32[8]{0:T(128)} %col_hbm.1, s32[8]{0:T(128)} %deal_hbm.1, ...), custom_call_target="tpu_custom_call" | custom-call | tf_op jit(solution)/shard_map/exchange/pallas_call | solution.py:231
  17.4 1.4 %gradient.1 = (bf16[1,512,1024]{2,1,0:T(8,128)(2,1)}, bf16[1,4096]{1,0:T(2,128)(2,1)}) custom-call(bf16[16,512]{1,0:T(8,128)(2,1)S(1)} %get-tuple-element.8.signal_ref, bf16[16,1024]{1,0:T(8,128)(2,1)S(1)} %get-tuple-element.9.source_ref, f32[1,1024]{1,0:T(1,128)S(1)} %get-tuple-element.10.scale_ref, bf16[1,4096]{1,0:T(2,128)(2,1)S(1)} %get-tuple-element.11.errors_ref), custom_call_target="tpu_custom_call" | custom-call | tf_op jit(solution)/shard_map/gradient/pallas_call | solution.py:268
